TPU v7x, 32 devices: a whole 2x2x4 slice. The times are simulated.
32 devices in a mesh: groups: 2 (over x), dp: 16 (over z, y, core).
Axes of the slice: x: 2, y: 2, z: 4, core: 2. Of those that a mesh axis runs over, the one named last changes fastest.
Arguments:
- tokens: bfloat16 [4096, 5120], P(('groups', 'dp')), parts along dimension 0, may hold values from -6 to 6
- cotangent: bfloat16 [4096, 5120], P(('groups', 'dp')), parts along dimension 0, may hold values from -6 to 6
- segments: int32 [32, 1, 3], P('groups'), parts along dimension 0, may hold values from 0 to 15, as said below
- owner_map: int32 [32], P('groups'), parts along dimension 0, may hold values from 0 to 15, each once
- down_t: bfloat16 [32, 64, 5120], P(('groups', 'dp')), parts along dimension 0, may hold values from -0.078125 to 0.078125
- up: bfloat16 [32, 64, 5120], P(('groups', 'dp')), parts along dimension 0, may hold values from -0.75 to 0.75
Outputs:
- grad_tokens: bfloat16 [4096, 5120], P(('groups', 'dp')), parts along dimension 0
- grad_down: bfloat16 [32, 64, 5120], P(('groups', 'dp')), parts along dimension 0
- grad_up: bfloat16 [32, 64, 5120], P(('groups', 'dp')), parts along dimension 0
There are 2 independent parts, one for each index of `groups`. A program takes and returns all parts, laid end to end along the dimension named above; each array names one. Nothing has to cross between parts.
Inputs may be any that keep to these rules, and one draw needn't show every extreme that they name: In segments[d] the live entries (count 1 or more) come first, cover blocks 0 to 0 in order without gaps, and the rest are (0, 0, 0); ids name adapters, some far more often than others.
All inputs are finite; a program needn't handle non-finite values.
Results may differ from a plain program's by a relative error of at most 0.0075.
Values may be sent and summed in bfloat16 or wider, within the bound.
No kernel may reach another device: no remote copies, remote signals or barrier semaphores. Data moves between devices by JAX's collectives and lax.ppermute only.
A program may use at most 64 MiB of HBM per device.

v0:
```python
import jax
import jax.numpy as jnp
from jax import lax
from jax.sharding import PartitionSpec as P

BLOCK = 128


def block_slots(segments, owner_map, blocks, count_adapters):
    index = jnp.arange(blocks, dtype=jnp.int32)
    ids = segments[:, :, 0]
    starts = segments[:, :, 1]
    counts = segments[:, :, 2]
    inside = (index[None, None, :] >= starts[:, :, None]) & (
        index[None, None, :] < (starts + counts)[:, :, None]
    )
    adapter = jnp.sum(jnp.where(inside, ids[:, :, None], 0), axis=1)
    match = adapter[:, :, None] == jnp.arange(count_adapters, dtype=jnp.int32)[None, None, :]
    slots = jnp.sum(jnp.where(match, owner_map[None, None, :], 0), axis=2)
    return slots.reshape(-1)


def slot_total(terms, slots, count_adapters):
    onehot = (slots[:, None] == jnp.arange(count_adapters, dtype=jnp.int32)[None, :]).astype(
        jnp.float32
    )
    return jnp.einsum("bk,brd->krd", onehot, terms)


def shards(tokens, cotangent, segments, owner_map, down_t, up):
    devices = lax.axis_size("dp")
    held = down_t.shape[0]
    count_adapters = held * devices
    blocks = tokens.shape[0] // BLOCK
    width = tokens.shape[1]
    narrow = width // devices
    slots = block_slots(segments, owner_map, blocks, count_adapters)
    scale = 1.0 / BLOCK
    table_down, table_up = (
        lax.all_to_all(down_t, "dp", split_axis=2, concat_axis=0, tiled=True),
        lax.all_to_all(up, "dp", split_axis=2, concat_axis=0, tiled=True),
    )
    send_down = jnp.take(table_down, slots, axis=0)
    send_up = jnp.take(table_up, slots, axis=0)
    mine_down, mine_up = (
        lax.all_to_all(send_down, "dp", split_axis=0, concat_axis=2, tiled=True),
        lax.all_to_all(send_up, "dp", split_axis=0, concat_axis=2, tiled=True),
    )
    rows = tokens.reshape(blocks, BLOCK, width)
    cots = cotangent.reshape(blocks, BLOCK, width)
    rows_split = tokens.reshape(blocks, BLOCK, devices, narrow)
    cots_split = cotangent.reshape(blocks, BLOCK, devices, narrow)
    hidden = jnp.einsum("btd,brd->btr", rows, mine_down, preferred_element_type=jnp.float32).astype(
        jnp.bfloat16
    )
    inner = jnp.einsum("btd,brd->btr", cots, mine_up, preferred_element_type=jnp.float32).astype(
        jnp.bfloat16
    )
    grad_rows = jnp.einsum(
        "btr,brd->btd", inner, mine_down, preferred_element_type=jnp.float32
    ).astype(jnp.bfloat16)
    term_down = (
        jnp.einsum("btr,btcd->cbrd", inner, rows_split, preferred_element_type=jnp.float32) * scale
    )
    term_up = (
        jnp.einsum("btr,btcd->cbrd", hidden, cots_split, preferred_element_type=jnp.float32) * scale
    )
    sliced_down, sliced_up = (
        lax.all_to_all(term_down, "dp", split_axis=0, concat_axis=0, tiled=True),
        lax.all_to_all(term_up, "dp", split_axis=0, concat_axis=0, tiled=True),
    )
    rank = inner.shape[2]
    summed_down = slot_total(
        sliced_down.reshape(devices * blocks, rank, narrow), slots, count_adapters
    )
    summed_up = slot_total(sliced_up.reshape(devices * blocks, rank, narrow), slots, count_adapters)
    grad_down, grad_up = (
        lax.all_to_all(
            summed_down.astype(jnp.bfloat16), "dp", split_axis=0, concat_axis=2, tiled=True
        ),
        lax.all_to_all(
            summed_up.astype(jnp.bfloat16), "dp", split_axis=0, concat_axis=2, tiled=True
        ),
    )
    return (grad_rows.reshape(blocks * BLOCK, width), grad_down, grad_up)


def solution(mesh):
    in_specs = (
        P(("groups", "dp"), None),
        P(("groups", "dp"), None),
        P("groups", None, None),
        P("groups"),
        P(("groups", "dp"), None, None),
        P(("groups", "dp"), None, None),
    )
    out_specs = (
        P(("groups", "dp"), None),
        P(("groups", "dp"), None, None),
        P(("groups", "dp"), None, None),
    )
    return jax.shard_map(shards, mesh=mesh, in_specs=in_specs, out_specs=out_specs, check_vma=False)
```

profile of v0, /device:TPU:0, one launch (start us, length us, event | category | flops | bytes accessed | tf_op | source)
XLA Modules:
  0.0 261.7 jit_solution(5187839497137100978)
XLA Ops:
  0.6 4.7 %copy.59 = bf16[1,64,5120]{1,0,2:T(2,128)(2,1)S(1)} copy(bf16[1,64,5120]{2,1,0:T(8,128)(2,1)} %param.13) | data formatting | bytes 1310720 | tf_op args[5]
  5.3 0.5 broadcast.107
  5.8 28.9 %reduce.2 = bf16[5120,64]{1,0:T(8,128)(2,1)} reduce(bf16[5120,1,64]{2,1,0:T(2,128)(2,1)S(1)} %bitcast.81, bf16[]{:T(256)} %broadcast.107), dimensions={1}, to_apply=%bitcast.69.reduce_sub_computation | reduce | bytes 1310722
  34.7 3.4 %reshape.176 = bf16[16,2,10240]{2,1,0:T(2,128)(2,1)} reshape(bf16[5120,64]{1,0:T(8,128)(2,1)} %reduce.2) | data formatting | bytes 1310720
  38.1 7.4 %all-to-all-start = ((bf16[16,2,10240]{2,1,0:T(2,128)(2,1)}), bf16[16,2,10240]{2,1,0:T(2,128)(2,1)S(1)}, u32[]{:S(2)}, u32[]{:S(2)}) async-start(bf16[16,2,10240]{2,1,0:T(2,128)(2,1)} %reshape.176), calls=%async_computation | async-start | bytes 1310720 | tf_op jit(solution)/shard_map/all_to_all | solution.py:41
  45.5 4.7 %copy.63 = bf16[1,64,5120]{1,0,2:T(2,128)(2,1)S(1)} copy(bf16[1,64,5120]{2,1,0:T(8,128)(2,1)} %param.12) | data formatting | bytes 1310720 | tf_op args[4]
  50.2 28.9 %reduce.1 = bf16[5120,64]{1,0:T(8,128)(2,1)} reduce(bf16[5120,1,64]{2,1,0:T(2,128)(2,1)S(1)} %bitcast.82, bf16[]{:T(256)} %broadcast.107), dimensions={1}, to_apply=%bitcast.71.reduce_sub_computation | reduce | bytes 1310722
  79.1 0.0 copy-start.5
  79.1 0.0 copy-start.6
  79.1 3.4 %reshape.178 = bf16[16,2,10240]{2,1,0:T(2,128)(2,1)} reshape(bf16[5120,64]{1,0:T(8,128)(2,1)} %reduce.1) | data formatting | bytes 1310720
  82.5 0.0 all-to-all-done
  82.5 6.0 %all-to-all-start.2 = ((bf16[16,2,10240]{2,1,0:T(2,128)(2,1)}), bf16[16,2,10240]{2,1,0:T(2,128)(2,1)}, u32[]{:S(2)}, u32[]{:S(2)}) async-start(bf16[16,2,10240]{2,1,0:T(2,128)(2,1)} %reshape.178), calls=%async_computation.2 | async-start | bytes 1310720 | tf_op jit(solution)/shard_map/all_to_all | solution.py:40
  88.5 0.0 copy-done.5
  88.6 0.0 copy-done.6
  88.6 0.2 select_reduce_fusion
  88.8 1.4 reshape.177
  90.2 1.2 copy.81
  91.4 1.7 copy.61
  93.1 12.1 %all-to-all-done.2 = bf16[16,2,10240]{2,1,0:T(2,128)(2,1)} async-done(((bf16[16,2,10240]{2,1,0:T(2,128)(2,1)}), bf16[16,2,10240]{2,1,0:T(2,128)(2,1)}, u32[]{:S(2)}, u32[]{:S(2)}) %all-to-all-start.2) | async-done | bytes 655392 | tf_op jit(solution)/shard_map/all_to_all | solution.py:40
  105.2 4.4 %reshape.179 = bf16[5120,1,64]{2,1,0:T(2,128)(2,1)S(1)} reshape(bf16[16,2,10240]{2,1,0:T(2,128)(2,1)} %all-to-all-done.2) | data formatting | bytes 1310720
  109.6 1.2 copy.82
  110.8 1.7 copy.65
  112.6 0.7 gather_fusion
  113.3 0.7 gather_fusion.1
  114.0 1.2 broadcast_select_fusion
  115.2 0.0 copy-start.1
  115.2 25.1 %all_to_all.112 = bf16[16,64,320]{2,1,0:T(8,128)(2,1)} all-to-all(bf16[16,64,320]{2,1,0:T(8,128)(2,1)S(1)} %get-tuple-element.5), channel_id=1, replica_groups=mesh['groups'=2,'dp'=16] {'dp'}, dimensions={0} | all-to-all | bytes 1310720 | tf_op jit(solution)/shard_map/all_to_all | solution.py:47
  140.2 3.9 %all-to-all-start.3 = ((bf16[16,64,320]{2,1,0:T(8,128)(2,1)}), bf16[16,64,320]{2,1,0:T(8,128)(2,1)S(1)}, u32[]{:S(2)}, u32[]{:S(2)}) async-start(bf16[16,64,320]{2,1,0:T(8,128)(2,1)} %get-tuple-element.4), calls=%async_computation.3 | async-start | bytes 1572864 | tf_op jit(solution)/shard_map/all_to_all | solution.py:46
  144.2 0.0 copy-done.1
  144.2 1.4 copy.67
  145.6 0.0 copy-start
  145.6 2.6 copy.62
  148.2 2.4 reshape.143
  150.6 0.0 copy-done
  150.6 0.0 copy-start.2
  150.6 1.8 convolution_convert_fusion.2
  152.4 0.0 copy-done.2
  152.4 1.6 multiply_bitcast_fusion.1
  154.0 8.9 %all-to-all-done.3 = bf16[16,64,320]{2,1,0:T(8,128)(2,1)S(1)} async-done(((bf16[16,64,320]{2,1,0:T(8,128)(2,1)}), bf16[16,64,320]{2,1,0:T(8,128)(2,1)S(1)}, u32[]{:S(2)}, u32[]{:S(2)}) %all-to-all-start.3) | async-done | bytes 655392 | tf_op jit(solution)/shard_map/all_to_all | solution.py:46
  162.9 0.0 copy-start.4
  162.9 5.5 %all-to-all-start.4 = ((bf16[16,1,64,320]{3,2,1,0:T(8,128)(2,1)}), bf16[16,1,64,320]{3,2,1,0:T(8,128)(2,1)}, u32[]{:S(2)}, u32[]{:S(2)}) async-start(bf16[16,1,64,320]{3,2,1,0:T(8,128)(2,1)} %multiply_bitcast_fusion.1), calls=%async_computation.4 | async-start | bytes 1572864 | tf_op jit(solution)/shard_map/all_to_all | solution.py:69
  168.4 1.4 copy.72
  169.8 0.0 copy-done.4
  169.8 0.0 copy-start.3
  169.8 2.6 copy.66
  172.4 1.8 reshape.144
  174.2 0.0 copy-done.3
  174.2 2.6 multiply_bitcast_fusion
  176.8 10.3 %all-to-all-done.4 = bf16[16,1,64,320]{3,2,1,0:T(8,128)(2,1)} async-done(((bf16[16,1,64,320]{3,2,1,0:T(8,128)(2,1)}), bf16[16,1,64,320]{3,2,1,0:T(8,128)(2,1)}, u32[]{:S(2)}, u32[]{:S(2)}) %all-to-all-start.4) | async-done | bytes 655392 | tf_op jit(solution)/shard_map/all_to_all | solution.py:69
  187.2 5.5 %all-to-all-start.6 = ((bf16[16,1,64,320]{3,2,1,0:T(8,128)(2,1)}), bf16[16,1,64,320]{3,2,1,0:T(8,128)(2,1)S(1)}, u32[]{:S(2)}, u32[]{:S(2)}) async-start(bf16[16,1,64,320]{3,2,1,0:T(8,128)(2,1)} %multiply_bitcast_fusion), calls=%async_computation.6 | async-start | bytes 1572864 | tf_op jit(solution)/shard_map/all_to_all | solution.py:70
  192.7 1.7 fusion.6
  194.4 1.1 copy.70
  195.4 15.9 %all-to-all-done.6 = bf16[16,1,64,320]{3,2,1,0:T(8,128)(2,1)S(1)} async-done(((bf16[16,1,64,320]{3,2,1,0:T(8,128)(2,1)}), bf16[16,1,64,320]{3,2,1,0:T(8,128)(2,1)S(1)}, u32[]{:S(2)}, u32[]{:S(2)}) %all-to-all-start.6) | async-done | bytes 655392 | tf_op jit(solution)/shard_map/all_to_all | solution.py:70
  211.4 5.5 %all-to-all-start.5 = ((bf16[16,64,320]{2,1,0:T(8,128)(2,1)}), bf16[16,64,320]{2,1,0:T(8,128)(2,1)S(1)}, u32[]{:S(2)}, u32[]{:S(2)}) async-start(bf16[16,64,320]{2,1,0:T(8,128)(2,1)} %copy.70), calls=%async_computation.5 | async-start | bytes 1572864 | tf_op jit(solution)/shard_map/all_to_all | solution.py:78
  216.8 0.6 fusion.9
  217.4 1.1 copy.75
  218.5 17.1 %all-to-all-done.5 = bf16[16,64,320]{2,1,0:T(8,128)(2,1)S(1)} async-done(((bf16[16,64,320]{2,1,0:T(8,128)(2,1)}), bf16[16,64,320]{2,1,0:T(8,128)(2,1)S(1)}, u32[]{:S(2)}, u32[]{:S(2)}) %all-to-all-start.5) | async-done | bytes 655392 | tf_op jit(solution)/shard_map/all_to_all | solution.py:78
  235.6 5.5 %all-to-all-start.7 = ((bf16[16,64,320]{2,1,0:T(8,128)(2,1)}), bf16[16,64,320]{2,1,0:T(8,128)(2,1)S(1)}, u32[]{:S(2)}, u32[]{:S(2)}) async-start(bf16[16,64,320]{2,1,0:T(8,128)(2,1)} %copy.75), calls=%async_computation.7 | async-start | bytes 1572864 | tf_op jit(solution)/shard_map/all_to_all | solution.py:81
  241.0 1.6 convolution_convert_fusion
  242.6 0.5 copy.71
  243.1 1.5 all_to_all.98
  244.6 15.2 %all-to-all-done.7 = bf16[16,64,320]{2,1,0:T(8,128)(2,1)S(1)} async-done(((bf16[16,64,320]{2,1,0:T(8,128)(2,1)}), bf16[16,64,320]{2,1,0:T(8,128)(2,1)S(1)}, u32[]{:S(2)}, u32[]{:S(2)}) %all-to-all-start.7) | async-done | bytes 655392 | tf_op jit(solution)/shard_map/all_to_all | solution.py:81
  259.7 0.5 copy.76
  260.2 1.5 all_to_all.103
  (4 shorter events, 0.0 us)
Async XLA Ops:
  38.1 44.4 %all-to-all-start = ((bf16[16,2,10240]{2,1,0:T(2,128)(2,1)}), bf16[16,2,10240]{2,1,0:T(2,128)(2,1)S(1)}, u32[]{:S(2)}, u32[]{:S(2)}) async-start(bf16[16,2,10240]{2,1,0:T(2,128)(2,1)} %reshape.176), calls=%async_computation | async-start | bytes 1310720 | tf_op jit(solution)/shard_map/all_to_all | solution.py:41
  79.1 9.4 %copy-start.5 = (s32[16,1,3]{0,1,2:T(1,128)S(1)}, s32[16,1,3]{0,1,2:T(1,128)}, u32[]{:S(2)}) copy-start(s32[16,1,3]{0,1,2:T(1,128)} %param.10) | copy-start | bytes 580
  79.1 9.5 %copy-start.6 = (s32[16]{0:T(128)S(1)}, s32[16]{0:T(128)}, u32[]{:S(2)}) copy-start(s32[16]{0:T(128)} %param.11) | copy-start | bytes 196
  82.5 22.7 %all-to-all-start.2 = ((bf16[16,2,10240]{2,1,0:T(2,128)(2,1)}), bf16[16,2,10240]{2,1,0:T(2,128)(2,1)}, u32[]{:S(2)}, u32[]{:S(2)}) async-start(bf16[16,2,10240]{2,1,0:T(2,128)(2,1)} %reshape.178), calls=%async_computation.2 | async-start | bytes 1310720 | tf_op jit(solution)/shard_map/all_to_all | solution.py:40
  115.2 29.0 %copy-start.1 = (bf16[128,5120]{1,0:T(8,128)(2,1)S(1)}, bf16[128,5120]{1,0:T(8,128)(2,1)}, u32[]{:S(2)}) copy-start(bf16[128,5120]{1,0:T(8,128)(2,1)} %param.8) | copy-start | bytes 3932164
  140.2 22.6 %all-to-all-start.3 = ((bf16[16,64,320]{2,1,0:T(8,128)(2,1)}), bf16[16,64,320]{2,1,0:T(8,128)(2,1)S(1)}, u32[]{:S(2)}, u32[]{:S(2)}) async-start(bf16[16,64,320]{2,1,0:T(8,128)(2,1)} %get-tuple-element.4), calls=%async_computation.3 | async-start | bytes 1572864 | tf_op jit(solution)/shard_map/all_to_all | solution.py:46
  145.6 5.0 %copy-start = (bf16[128,5120]{1,0:T(8,128)(2,1)S(1)}, bf16[128,5120]{1,0:T(8,128)(2,1)}, u32[]{:S(2)}) copy-start(bf16[128,5120]{1,0:T(8,128)(2,1)} %param.9) | copy-start | bytes 3932164
  150.6 1.8 copy-start.2
  162.9 7.0 %copy-start.4 = (bf16[16,64,320]{2,1,0:T(8,128)(2,1)}, bf16[16,64,320]{2,1,0:T(8,128)(2,1)S(1)}, u32[]{:S(2)}) copy-start(bf16[16,64,320]{2,1,0:T(8,128)(2,1)S(1)} %all-to-all-done.3) | copy-start | bytes 1966084
  162.9 24.3 %all-to-all-start.4 = ((bf16[16,1,64,320]{3,2,1,0:T(8,128)(2,1)}), bf16[16,1,64,320]{3,2,1,0:T(8,128)(2,1)}, u32[]{:S(2)}, u32[]{:S(2)}) async-start(bf16[16,1,64,320]{3,2,1,0:T(8,128)(2,1)} %multiply_bitcast_fusion.1), calls=%async_computation.4 | async-start | bytes 1572864 | tf_op jit(solution)/shard_map/all_to_all | solution.py:69
  169.8 4.4 %copy-start.3 = (bf16[128,5120]{0,1:T(8,128)(2,1)S(1)}, bf16[128,5120]{0,1:T(8,128)(2,1)}, u32[]{:S(2)}) copy-start(bf16[128,5120]{0,1:T(8,128)(2,1)} %copy.72) | copy-start | bytes 3932164
  187.2 24.2 %all-to-all-start.6 = ((bf16[16,1,64,320]{3,2,1,0:T(8,128)(2,1)}), bf16[16,1,64,320]{3,2,1,0:T(8,128)(2,1)S(1)}, u32[]{:S(2)}, u32[]{:S(2)}) async-start(bf16[16,1,64,320]{3,2,1,0:T(8,128)(2,1)} %multiply_bitcast_fusion), calls=%async_computation.6 | async-start | bytes 1572864 | tf_op jit(solution)/shard_map/all_to_all | solution.py:70
  211.4 24.2 %all-to-all-start.5 = ((bf16[16,64,320]{2,1,0:T(8,128)(2,1)}), bf16[16,64,320]{2,1,0:T(8,128)(2,1)S(1)}, u32[]{:S(2)}, u32[]{:S(2)}) async-start(bf16[16,64,320]{2,1,0:T(8,128)(2,1)} %copy.70), calls=%async_computation.5 | async-start | bytes 1572864 | tf_op jit(solution)/shard_map/all_to_all | solution.py:78
  235.6 24.2 %all-to-all-start.7 = ((bf16[16,64,320]{2,1,0:T(8,128)(2,1)}), bf16[16,64,320]{2,1,0:T(8,128)(2,1)S(1)}, u32[]{:S(2)}, u32[]{:S(2)}) async-start(bf16[16,64,320]{2,1,0:T(8,128)(2,1)} %copy.75), calls=%async_computation.7 | async-start | bytes 1572864 | tf_op jit(solution)/shard_map/all_to_all | solution.py:81
where the time goes:
time: 263 us; the launch traced here: 262 us
  waiting for transfers between devices  79.5 us (30%)
  other arithmetic  59.2 us (23%)
  local copies, waits for them, and re-layouts  48 us (18%)
  starting transfers between devices  39.3 us (15%)
  blocking collectives  25.1 us (10%)
  matrix products  9.78 us (4%)
    unnamed x2, other arithmetic  57.8 us
    unnamed x25, local copies, waits for them, and re-layouts  27.8 us
    all_to_all x1, blocking collectives, shards(): lax.all_to_all(send_up, 'dp', split_axis=0, concat_axis=2, tiled=True)  25.1 us
    all_to_all x1, waiting for transfers between devices, shards(): lax.all_to_all(summed_down.astype(jnp.bfloat16), 'dp', split_axis=0, conc...  17.1 us
    all_to_all x1, waiting for transfers between devices, shards(): lax.all_to_all(term_up, 'dp', split_axis=0, concat_axis=0, tiled=True)  15.9 us
    all_to_all x1, waiting for transfers between devices, shards(): lax.all_to_all(summed_up.astype(jnp.bfloat16), 'dp', split_axis=0, concat...  15.2 us
    all_to_all x1, waiting for transfers between devices, shards(): lax.all_to_all(down_t, 'dp', split_axis=2, concat_axis=0, tiled=True)  12.1 us
    all_to_all x1, waiting for transfers between devices, shards(): lax.all_to_all(term_down, 'dp', split_axis=0, concat_axis=0, tiled=True)  10.3 us
  transfers between devices with their start and end apart: 7, of which 6 were waited for; matrix products, arithmetic and copies ran while one was open for 25% of the time, Pallas kernels for 0%

commit v1 on v0

v1 whole, which is shorter than its diff:
```python
import jax
import jax.numpy as jnp
from jax import lax
from jax.sharding import PartitionSpec as P

BLOCK = 128


def block_slots(segments, owner_map, blocks, count_adapters):
    index = jnp.arange(blocks, dtype=jnp.int32)
    ids = segments[:, :, 0]
    starts = segments[:, :, 1]
    counts = segments[:, :, 2]
    inside = (index[None, None, :] >= starts[:, :, None]) & (
        index[None, None, :] < (starts + counts)[:, :, None]
    )
    adapter = jnp.sum(jnp.where(inside, ids[:, :, None], 0), axis=1)
    match = adapter[:, :, None] == jnp.arange(count_adapters, dtype=jnp.int32)[None, None, :]
    slots = jnp.sum(jnp.where(match, owner_map[None, None, :], 0), axis=2)
    return slots.reshape(-1)


def shards(tokens, cotangent, segments, owner_map, down_t, up):
    devices = lax.axis_size("dp")
    width = tokens.shape[1]
    rank = down_t.shape[1]
    slots = block_slots(segments, owner_map, 1, devices)
    scale = 1.0 / BLOCK
    piece = 2 * rank // devices
    stack = jnp.concatenate([down_t[0], up[0]], axis=0).reshape(devices, piece, width)
    table = lax.all_to_all(stack, "dp", split_axis=0, concat_axis=0, tiled=True)
    chosen = jnp.take(table, slots, axis=0, mode="clip")
    mine = lax.all_to_all(chosen, "dp", split_axis=0, concat_axis=0, tiled=True)
    mine = mine.reshape(2 * rank, width)
    down, up_ = mine[:rank], mine[rank:]
    f32 = jnp.float32
    hidden = jnp.einsum("td,rd->tr", tokens, down, preferred_element_type=f32).astype(jnp.bfloat16)
    inner = jnp.einsum("td,rd->tr", cotangent, up_, preferred_element_type=f32).astype(jnp.bfloat16)
    term_down = jnp.einsum("tr,td->rd", inner, tokens, preferred_element_type=f32)
    term_up = jnp.einsum("tr,td->rd", hidden, cotangent, preferred_element_type=f32)
    terms = jnp.concatenate([term_down, term_up], axis=0).astype(jnp.bfloat16)
    grad_rows = jnp.einsum("tr,rd->td", inner, down, preferred_element_type=f32).astype(jnp.bfloat16)
    pieces = lax.all_to_all(
        terms.reshape(devices, piece, width), "dp", split_axis=0, concat_axis=0, tiled=True
    )
    onehot = (slots[None, :] == jnp.arange(devices, dtype=jnp.int32)[:, None]).astype(jnp.bfloat16)
    summed = jnp.einsum("kb,bpd->kpd", onehot, pieces, preferred_element_type=f32) * scale
    grads = lax.all_to_all(
        summed.astype(jnp.bfloat16), "dp", split_axis=0, concat_axis=0, tiled=True
    ).reshape(2, rank, width)
    return grad_rows, grads[:1], grads[1:]


def solution(mesh):
    in_specs = (
        P(("groups", "dp"), None),
        P(("groups", "dp"), None),
        P("groups", None, None),
        P("groups"),
        P(("groups", "dp"), None, None),
        P(("groups", "dp"), None, None),
    )
    out_specs = (
        P(("groups", "dp"), None),
        P(("groups", "dp"), None, None),
        P(("groups", "dp"), None, None),
    )
    return jax.shard_map(shards, mesh=mesh, in_specs=in_specs, out_specs=out_specs, check_vma=False)
```

time: 263 us -> 161 us (0.61)
  other arithmetic: 59.2 us -> 3.9 us
  blocking collectives: 25.1 us -> 75 us
  local copies, waits for them, and re-layouts: 48 us -> 5.93 us
  starting transfers between devices: 39.3 us -> 11.9 us
  waiting for transfers between devices: 79.5 us -> 53 us
    unnamed x2 -> x0, other arithmetic: 57.8 us -> none
    all_to_all x1 -> x2, blocking collectives: 25.1 us -> 75 us  [the longest x1 39.7 us: shards(): mine = lax.all_to_all(chosen, 'dp', split_axis=0, concat_axis=0, tiled=True)]
    unnamed x25 -> x8, local copies, waits for them, and re-layouts: 27.8 us -> 0.02 us
    all_to_all x7 -> x2, starting transfers between devices: 39.3 us -> 11.9 us  [the longest x1 7.52 us: shards(): table = lax.all_to_all(stack, 'dp', split_axis=0, concat_axis=0, tiled=True)]
    all_to_all x7 -> x2, waiting for transfers between devices: 79.5 us -> 53 us  [the longest x1 27.2 us: shards(): table = lax.all_to_all(stack, 'dp', split_axis=0, concat_axis=0, tiled=True)]
    all_to_all x8 -> x0, local copies, waits for them, and re-layouts: 12.4 us -> none  [the longest x1 2.58 us: shards(): lax.all_to_all(send_down, 'dp', split_axis=0, concat_axis=2, tiled=True)]
    another operation x2 -> x0, local copies, waits for them, and re-layouts: 4.19 us -> none
    dot_general x6 -> x5, matrix products: 9.78 us -> 7.34 us  [the longest x1 3.29 us: shards(): jnp.einsum('tr,td->rd', hidden, cotangent, preferred_element_type=f32)]
  transfers between devices with their start and end apart: 7 -> 2, of which waited for: 6 -> 2; matrix products, arithmetic and copies ran while one was open for 25% -> 1% of each run, Pallas kernels for 0% -> 0%
where the time goes in v1:
time: 161 us; the launch traced here: 158 us
  blocking collectives  75 us (47%)
  waiting for transfers between devices  53 us (33%)
  starting transfers between devices  11.9 us (7%)
  matrix products  7.34 us (5%)
  local copies, waits for them, and re-layouts  5.93 us (4%)
  other arithmetic  3.9 us (2%)
    all_to_all x1, blocking collectives, shards(): mine = lax.all_to_all(chosen, 'dp', split_axis=0, concat_axis=0, tiled=True)  39.7 us
    all_to_all x1, blocking collectives, shards(): lax.all_to_all(terms.reshape(devices, piece, width), 'dp', split_axis=0,...  35.3 us
    all_to_all x1, waiting for transfers between devices, shards(): table = lax.all_to_all(stack, 'dp', split_axis=0, concat_axis=0, tiled=True)  27.2 us
    all_to_all x1, waiting for transfers between devices, shards(): lax.all_to_all(summed.astype(jnp.bfloat16), 'dp', split_axis=0, concat_ax...  25.8 us
    all_to_all x1, starting transfers between devices, shards(): table = lax.all_to_all(stack, 'dp', split_axis=0, concat_axis=0, tiled=True)  7.52 us
    all_to_all x1, starting transfers between devices, shards(): lax.all_to_all(summed.astype(jnp.bfloat16), 'dp', split_axis=0, concat_ax...  4.39 us
    dot_general x1, matrix products, shards(): jnp.einsum('tr,td->rd', hidden, cotangent, preferred_element_type=f32)  3.29 us
  transfers between devices with their start and end apart: 2, of which 2 were waited for; matrix products, arithmetic and copies ran while one was open for 1% of the time, Pallas kernels for 0%

profile of v1, /device:TPU:0, one launch (start us, length us, event | category | flops | bytes accessed | tf_op | source)
XLA Modules:
  0.0 157.7 jit_solution(13561149133828881503)
XLA Ops:
  0.6 0.0 copy-start
  0.6 2.5 %maximum_bitcast_fusion = bf16[16,8,5120]{2,1,0:T(8,128)(2,1)} fusion(bf16[64,5120]{1,0:T(8,128)(2,1)} %bitcast.29, bf16[64,5120]{1,0:T(8,128)(2,1)} %bitcast.30), kind=kLoop, calls=%fused_computation.6 | loop fusion | flops 2621440 | bytes 2621440 | tf_op jit(solution)/shard_map/reshape | solution.py:30
  3.2 0.0 copy-start.2
  3.2 0.0 copy-start.3
  3.2 7.5 %all-to-all-start = ((bf16[16,8,5120]{2,1,0:T(8,128)(2,1)}), bf16[16,8,5120]{2,1,0:T(8,128)(2,1)S(1)}, u32[]{:S(2)}, u32[]{:S(2)}) async-start(bf16[16,8,5120]{2,1,0:T(8,128)(2,1)} %maximum_bitcast_fusion), calls=%async_computation | async-start | bytes 2621440 | tf_op jit(solution)/shard_map/all_to_all | solution.py:31
  10.7 0.0 copy-done.2
  10.7 0.0 copy-done.3
  10.7 0.2 select_reduce_fusion
  10.9 27.2 %all-to-all-done = bf16[16,8,5120]{2,1,0:T(8,128)(2,1)S(1)} async-done(((bf16[16,8,5120]{2,1,0:T(8,128)(2,1)}), bf16[16,8,5120]{2,1,0:T(8,128)(2,1)S(1)}, u32[]{:S(2)}, u32[]{:S(2)}) %all-to-all-start) | async-done | bytes 1310752 | tf_op jit(solution)/shard_map/all_to_all | solution.py:31
  38.1 1.7 %gather_fusion = bf16[16,8,5120]{2,1,0:T(8,128)(2,1)} fusion(bf16[16,8,5120]{2,1,0:T(8,128)(2,1)S(1)} %all-to-all-done, s32[1024]{0:T(1024)S(1)} %pad_clamp_fusion), kind=kCustom, calls=%fused_computation | custom fusion | bytes 2621504 | tf_op jit(solution)/shard_map/jit(_take)/gather | solution.py:32
  39.8 0.0 copy-start.1
  39.8 39.7 %all_to_all.20 = bf16[16,8,5120]{2,1,0:T(8,128)(2,1)S(1)} all-to-all(bf16[16,8,5120]{2,1,0:T(8,128)(2,1)} %gather_fusion), channel_id=1, replica_groups=mesh['groups'=2,'dp'=16] {'dp'}, dimensions={0} | all-to-all | bytes 2621440 | tf_op jit(solution)/shard_map/all_to_all | solution.py:33
  79.5 0.0 copy-done.1
  79.5 0.6 convolution_convert_fusion.4
  80.0 0.0 copy-done
  80.1 0.3 convolution_convert_fusion.2
  80.4 3.3 %convolution_convert_fusion.1 = bf16[64,5120]{1,0:T(8,128)(2,1)} fusion(bf16[128,5120]{1,0:T(8,128)(2,1)} %param.7, bf16[128,5120]{1,0:T(8,128)(2,1)S(1)} %copy-done, bf16[16,8,5120]{2,1,0:T(8,128)(2,1)S(1)} %all_to_all.20), kind=kOutput, calls=%fused_computation.4 | convolution fusion | flops 168108032 | bytes 3932160 | tf_op jit(solution)/shard_map/tr,td->rd/dot_general | solution.py:40
  83.7 1.2 maximum_bitcast_fusion.1
  84.9 35.3 %all_to_all.21 = bf16[16,8,5120]{2,1,0:T(8,128)(2,1)S(1)} all-to-all(bf16[16,8,5120]{2,1,0:T(8,128)(2,1)S(1)} %maximum_bitcast_fusion.1), channel_id=1, replica_groups=mesh['groups'=2,'dp'=16] {'dp'}, dimensions={0} | all-to-all | bytes 2621440 | tf_op jit(solution)/shard_map/all_to_all | solution.py:43
  120.2 1.6 fusion
  121.7 1.8 %copy.16 = bf16[16,8,5120]{2,1,0:T(8,128)(2,1)} copy(bf16[16,8,5120]{2,0,1:T(8,128)(2,1)S(1)} %fusion) | data formatting | bytes 2621440 | tf_op jit(solution)/shard_map/convert_element_type | solution.py:49
  123.5 4.4 %all-to-all-start.3 = ((bf16[16,8,5120]{2,1,0:T(8,128)(2,1)}), bf16[16,8,5120]{2,1,0:T(8,128)(2,1)}, u32[]{:S(2)}, u32[]{:S(2)}) async-start(bf16[16,8,5120]{2,1,0:T(8,128)(2,1)} %copy.16), calls=%async_computation.3 | async-start | bytes 2621440 | tf_op jit(solution)/shard_map/all_to_all | solution.py:48
  127.9 1.6 %convolution_convert_fusion = bf16[128,5120]{1,0:T(8,128)(2,1)} fusion(bf16[64,128]{1,0:T(8,128)(2,1)S(1)} %convolution_convert_fusion.4, bf16[16,8,5120]{2,1,0:T(8,128)(2,1)S(1)} %all_to_all.20), kind=kOutput, calls=%fused_computation.3 | convolution fusion | flops 84541440 | bytes 1982464 | tf_op jit(solution)/shard_map/tr,rd->td/dot_general | solution.py:42
  129.5 25.8 %all-to-all-done.3 = bf16[16,8,5120]{2,1,0:T(8,128)(2,1)} async-done(((bf16[16,8,5120]{2,1,0:T(8,128)(2,1)}), bf16[16,8,5120]{2,1,0:T(8,128)(2,1)}, u32[]{:S(2)}, u32[]{:S(2)}) %all-to-all-start.3) | async-done | bytes 1310752 | tf_op jit(solution)/shard_map/all_to_all | solution.py:48
  155.3 2.4 %slice_bitcast_fusion = (bf16[1,64,5120]{2,1,0:T(8,128)(2,1)}, bf16[1,64,5120]{2,1,0:T(8,128)(2,1)}) fusion(bf16[16,8,5120]{2,1,0:T(8,128)(2,1)} %all-to-all-done.3), kind=kLoop, calls=%fused_computation.11 | loop fusion | bytes 2621440 | tf_op jit(solution)/shard_map/slice | solution.py:51
  (2 shorter events, 0.0 us)
Async XLA Ops:
  0.6 79.4 %copy-start = (bf16[128,5120]{1,0:T(8,128)(2,1)S(1)}, bf16[128,5120]{1,0:T(8,128)(2,1)}, u32[]{:S(2)}) copy-start(bf16[128,5120]{1,0:T(8,128)(2,1)} %param.6) | copy-start | bytes 3932164
  3.2 7.5 %copy-start.2 = (s32[16,1,3]{0,1,2:T(1,128)S(1)}, s32[16,1,3]{0,1,2:T(1,128)}, u32[]{:S(2)}) copy-start(s32[16,1,3]{0,1,2:T(1,128)} %param.8) | copy-start | bytes 580
  3.2 7.6 %copy-start.3 = (s32[16]{0:T(128)S(1)}, s32[16]{0:T(128)}, u32[]{:S(2)}) copy-start(s32[16]{0:T(128)} %param.9) | copy-start | bytes 196
  3.2 34.9 %all-to-all-start = ((bf16[16,8,5120]{2,1,0:T(8,128)(2,1)}), bf16[16,8,5120]{2,1,0:T(8,128)(2,1)S(1)}, u32[]{:S(2)}, u32[]{:S(2)}) async-start(bf16[16,8,5120]{2,1,0:T(8,128)(2,1)} %maximum_bitcast_fusion), calls=%async_computation | async-start | bytes 2621440 | tf_op jit(solution)/shard_map/all_to_all | solution.py:31
  39.8 39.7 %copy-start.1 = (bf16[128,5120]{1,0:T(8,128)(2,1)S(1)}, bf16[128,5120]{1,0:T(8,128)(2,1)}, u32[]{:S(2)}) copy-start(bf16[128,5120]{1,0:T(8,128)(2,1)} %param.7) | copy-start | bytes 3932164
  123.5 31.8 %all-to-all-start.3 = ((bf16[16,8,5120]{2,1,0:T(8,128)(2,1)}), bf16[16,8,5120]{2,1,0:T(8,128)(2,1)}, u32[]{:S(2)}, u32[]{:S(2)}) async-start(bf16[16,8,5120]{2,1,0:T(8,128)(2,1)} %copy.16), calls=%async_computation.3 | async-start | bytes 2621440 | tf_op jit(solution)/shard_map/all_to_all | solution.py:48

commit v2 on v1

v2 whole, which is shorter than its diff:
```python
import functools

import jax
import jax.numpy as jnp
from jax import lax
from jax.experimental import pallas as pl
from jax.experimental.pallas import tpu as pltpu
from jax.sharding import PartitionSpec as P

BLOCK = 128
F32 = jnp.float32
BF16 = jnp.bfloat16
I32 = jnp.int32


def block_slots(segments, owner_map, blocks, count_adapters):
    index = jnp.arange(blocks, dtype=I32)
    ids = segments[:, :, 0]
    starts = segments[:, :, 1]
    counts = segments[:, :, 2]
    inside = (index[None, None, :] >= starts[:, :, None]) & (
        index[None, None, :] < (starts + counts)[:, :, None]
    )
    adapter = jnp.sum(jnp.where(inside, ids[:, :, None], 0), axis=1)
    match = adapter[:, :, None] == jnp.arange(count_adapters, dtype=I32)[None, None, :]
    slots = jnp.sum(jnp.where(match, owner_map[None, None, :], 0), axis=2)
    return slots.reshape(-1)


def padded(shape, itemsize):
    rows = -(-shape[-2] // 16) * 16
    size = rows * shape[-1] * itemsize
    for extent in shape[:-2]:
        size *= extent
    return size


def vmem(shapes):
    return pltpu.CompilerParams(
        vmem_limit_bytes=sum(padded(shape, size) for shape, size in shapes) + (4 << 20)
    )


def select_pieces(index, sources, count):
    shape = (count,) + sources[0].shape[1:]
    sizes = [source.shape[0] for source in sources]

    def kernel(index_ref, *refs):
        out_ref = refs[-1]

        def body(j, carry):
            place = index_ref[j]
            low = 0
            for size, ref in zip(sizes, refs[:-1]):

                @pl.when((place >= low) & (place < low + size))
                def _(ref=ref, low=low):
                    out_ref[j] = ref[place - low]

                low += size
            return carry

        lax.fori_loop(0, count, body, 0)

    whole = pl.BlockSpec(memory_space=pltpu.VMEM)
    return pl.pallas_call(
        kernel,
        out_shape=jax.ShapeDtypeStruct(shape, sources[0].dtype),
        in_specs=[pl.BlockSpec(memory_space=pltpu.SMEM)] + [whole] * len(sources),
        out_specs=whole,
        compiler_params=vmem([(source.shape, 2) for source in sources] + [(shape, 2)]),
    )(index, *sources)


def sum_pieces(indices, sources, count, scale):
    shape = (count,) + sources[0].shape[1:]
    total_shape = (count + 1,) + sources[0].shape[1:]
    many = len(sources)

    def kernel(*refs):
        index_refs, source_refs = refs[:many], refs[many : 2 * many]
        out_ref, total_ref = refs[2 * many :]
        total_ref[...] = jnp.zeros_like(total_ref)
        for index_ref, source_ref in zip(index_refs, source_refs):

            def body(d, carry, index_ref=index_ref, source_ref=source_ref):
                place = index_ref[d]
                total_ref[place] = total_ref[place] + source_ref[d].astype(F32)
                return carry

            lax.fori_loop(0, source_ref.shape[0], body, 0)

        def finish(k, carry):
            out_ref[k] = (total_ref[k] * scale).astype(BF16)
            return carry

        lax.fori_loop(0, count, finish, 0)

    whole = pl.BlockSpec(memory_space=pltpu.VMEM)
    return pl.pallas_call(
        kernel,
        out_shape=jax.ShapeDtypeStruct(shape, BF16),
        in_specs=[pl.BlockSpec(memory_space=pltpu.SMEM)] * many + [whole] * many,
        out_specs=whole,
        scratch_shapes=[pltpu.VMEM(total_shape, F32)],
        compiler_params=vmem(
            [(source.shape, 2) for source in sources] + [(shape, 2), (total_shape, 4)]
        ),
    )(*indices, *sources)


def dot(spec, a, b):
    return jnp.einsum(spec, a, b, preferred_element_type=F32)


def two_step(slots, tokens, cotangent, down_t, up):
    devices = lax.axis_size("dp")
    rank, width = down_t.shape[1:]
    piece = 2 * rank // devices
    exchange = functools.partial(
        lax.all_to_all, axis_name="dp", split_axis=0, concat_axis=0, tiled=True
    )
    stack = jnp.concatenate([down_t[0], up[0]], axis=0).reshape(devices, piece, width)
    table = exchange(stack)
    mine = exchange(jnp.take(table, slots, axis=0, mode="clip")).reshape(2 * rank, width)
    down, up_ = mine[:rank], mine[rank:]
    hidden = dot("td,rd->tr", tokens, down).astype(BF16)
    inner = dot("td,rd->tr", cotangent, up_).astype(BF16)
    grad_rows = dot("tr,rd->td", inner, down).astype(BF16)
    terms = jnp.concatenate(
        [dot("tr,td->rd", inner, tokens), dot("tr,td->rd", hidden, cotangent)], axis=0
    ).astype(BF16)
    pieces = exchange(terms.reshape(devices, piece, width))
    onehot = (slots[None, :] == jnp.arange(devices, dtype=I32)[:, None]).astype(BF16)
    summed = dot("kb,bpd->kpd", onehot, pieces) * (1.0 / BLOCK)
    grads = exchange(summed.astype(BF16)).reshape(2, rank, width)
    return grad_rows, grads[:1], grads[1:]


def crossing(slots, devices):
    half = devices // 2
    k = jnp.arange(devices, dtype=I32)
    side = k // half
    uses = slots[:, None] == k[None, :]
    need = jnp.any(uses & (side[:, None] != side[None, :]), axis=0)
    before = need[None, :] & (side[None, :] == side[:, None]) & (k[None, :] < k[:, None])
    place = jnp.sum(before.astype(I32), axis=1)
    counts = jnp.stack([jnp.sum(need[:half].astype(I32)), jnp.sum(need[half:].astype(I32))])
    return need, place, counts


def three_step(capacity, slots, need, place, counts, tokens, cotangent, down_t, up):
    devices = lax.axis_size("dp")
    half = devices // 2
    rank, width = down_t.shape[1:]
    piece = rank // half
    groups = [list(range(half)), list(range(half, devices))]
    pairs = [(i, (i + half) % devices) for i in range(devices)]
    exchange = functools.partial(
        lax.all_to_all,
        axis_name="dp",
        split_axis=0,
        concat_axis=0,
        tiled=True,
        axis_index_groups=groups,
    )
    cross = functools.partial(lax.ppermute, axis_name="dp", perm=pairs)
    side = lax.axis_index("dp") // half
    k = jnp.arange(half, dtype=I32)
    j = jnp.arange(capacity, dtype=I32)
    my_need = lax.dynamic_slice(need, (side * half,), (half,))
    my_place = lax.dynamic_slice(place, (side * half,), (half,))
    my_count = lax.dynamic_slice(counts, (side,), (1,))
    my_slots = lax.dynamic_slice(slots, (side * half,), (half,))
    match = my_need[None, :] & (my_place[None, :] == j[:, None])
    send = jnp.sum(jnp.where(match, k[None, :], 0), axis=1)
    local = my_slots // half == side
    slot_place = jnp.sum(
        jnp.where(my_slots[:, None] == jnp.arange(devices, dtype=I32)[None, :], place[None, :], 0),
        axis=1,
    )
    fetch = jnp.where(local, my_slots % half, half + slot_place)
    to_cross = jnp.where(local, capacity, slot_place)
    to_local = jnp.where(local, my_slots % half, half)
    to_arrived = jnp.where(j < my_count, send, half)

    def spread(adapter):
        return exchange(adapter.reshape(half, piece, width))

    def send_across(table):
        return cross(select_pieces(send, [table], capacity))

    def gather(table, arrived):
        return exchange(select_pieces(fetch, [table, arrived], half)).reshape(rank, width)

    def sums_across(pieces):
        return cross(sum_pieces([to_cross], [pieces], capacity, 1.0))

    def collect(pieces, arrived):
        summed = sum_pieces([to_local, to_arrived], [pieces, arrived], half, 1.0 / BLOCK)
        return exchange(summed).reshape(1, rank, width)

    table_down = spread(down_t)
    arrived_down = send_across(table_down)
    table_up = spread(up)
    arrived_up = send_across(table_up)
    down = gather(table_down, arrived_down)
    hidden = dot("td,rd->tr", tokens, down).astype(BF16)
    term_up = dot("tr,td->rd", hidden, cotangent).astype(BF16)
    up_ = gather(table_up, arrived_up)
    pieces_up = spread(term_up)
    inner = dot("td,rd->tr", cotangent, up_).astype(BF16)
    term_down = dot("tr,td->rd", inner, tokens).astype(BF16)
    sums_up = sums_across(pieces_up)
    pieces_down = spread(term_down)
    sums_down = sums_across(pieces_down)
    grad_rows = dot("tr,rd->td", inner, down).astype(BF16)
    grad_up = collect(pieces_up, sums_up)
    grad_down = collect(pieces_down, sums_down)
    return grad_rows, grad_down, grad_up


def shards(tokens, cotangent, segments, owner_map, down_t, up):
    devices = lax.axis_size("dp")
    slots = block_slots(segments, owner_map, 1, devices)
    need, place, counts = crossing(slots, devices)
    capacity = devices // 4

    def few(*args):
        return three_step(capacity, slots, need, place, counts, *args)

    def many(*args):
        return two_step(slots, *args)

    return lax.cond(jnp.max(counts) <= capacity, few, many, tokens, cotangent, down_t, up)


def solution(mesh):
    in_specs = (
        P(("groups", "dp"), None),
        P(("groups", "dp"), None),
        P("groups", None, None),
        P("groups"),
        P(("groups", "dp"), None, None),
        P(("groups", "dp"), None, None),
    )
    out_specs = (
        P(("groups", "dp"), None),
        P(("groups", "dp"), None, None),
        P(("groups", "dp"), None, None),
    )
    return jax.shard_map(shards, mesh=mesh, in_specs=in_specs, out_specs=out_specs, check_vma=False)
```

time: 161 us -> 166 us (1.031); the launches traced: 158 us -> 165 us
  blocking collectives: 75 us -> 16.1 us
  starting transfers between devices: 11.9 us -> 47.6 us
  waiting for transfers between devices: 53 us -> 72.1 us
  Pallas kernels: 0 us -> 9.58 us
    all_to_all x2 -> x1, blocking collectives: 75 us -> 16.1 us  [spread(): return exchange(adapter.reshape(half, piece, width))]
    ppermute x0 -> x4, waiting for transfers between devices: none -> 47.7 us  [the longest x2 26.8 us: send_across(): return cross(select_pieces(send, [table], capacity))]
    all_to_all x2 -> x7, waiting for transfers between devices: 53 us -> 24.4 us  [the longest x2 9.09 us: collect(): return exchange(summed).reshape(1, rank, width)]
    all_to_all x2 -> x7, starting transfers between devices: 11.9 us -> 35.3 us  [the longest x2 14.4 us: collect(): return exchange(summed).reshape(1, rank, width)]
    ppermute x0 -> x4, starting transfers between devices: none -> 12.3 us  [the longest x2 6.65 us: sums_across(): return cross(sum_pieces([to_cross], [pieces], capacity, 1.0))]
    pallas_call x0 -> x8, Pallas kernels: none -> 9.58 us  [the longest x4 5.21 us: sum_pieces(): pl.pallas_call(kernel, out_shape=jax.ShapeDtypeStruct(shape, BF16), in_sp...]
    unnamed x8 -> x2, local copies, waits for them, and re-layouts: 0.02 us -> 3.93 us
    reshape x1 -> x0, other arithmetic: 2.53 us -> none  [shards(): jnp.concatenate([down_t[0], up[0]], axis=0).reshape(devices, piece, width)]
  transfers between devices with their start and end apart: 2 -> 11, of which waited for: 2 -> 10; matrix products, arithmetic and copies ran while one was open for 1% -> 5% of each run, Pallas kernels for 0% -> 6%
where the time goes in v2:
time: 166 us; the launch traced here: 165 us
  waiting for transfers between devices  72.1 us (43%)
  starting transfers between devices  47.6 us (29%)
  blocking collectives  16.1 us (10%)
  Pallas kernels  9.58 us (6%)
  matrix products  6.63 us (4%)
  local copies, waits for them, and re-layouts  5.47 us (3%)
  other arithmetic  4.93 us (3%)
  between operations  1.94 us (1%)
    ppermute x2, waiting for transfers between devices, send_across(): return cross(select_pieces(send, [table], capacity))  26.8 us
    ppermute x2, waiting for transfers between devices, sums_across(): return cross(sum_pieces([to_cross], [pieces], capacity, 1.0))  20.9 us
    all_to_all x1, blocking collectives, spread(): return exchange(adapter.reshape(half, piece, width))  16.1 us
    all_to_all x2, starting transfers between devices, collect(): return exchange(summed).reshape(1, rank, width)  14.4 us
    all_to_all x3, starting transfers between devices, spread(): return exchange(adapter.reshape(half, piece, width))  10.6 us
    all_to_all x2, starting transfers between devices, gather(): exchange(select_pieces(fetch, [table, arrived], half)).reshape(rank, width)  10.3 us
    all_to_all x2, waiting for transfers between devices, collect(): return exchange(summed).reshape(1, rank, width)  9.09 us
    all_to_all x3, waiting for transfers between devices, spread(): return exchange(adapter.reshape(half, piece, width))  7.91 us
  transfers between devices with their start and end apart: 11, of which 10 were waited for; matrix products, arithmetic and copies ran while one was open for 5% of the time, Pallas kernels for 6%

profile of v2, /device:TPU:0, one launch (start us, length us, event | category | flops | bytes accessed | tf_op | source)
XLA Modules:
  0.0 164.6 jit_solution(8839981269829329221)
XLA Ops:
  0.6 0.7 fusion.21
  1.3 0.8 select_reduce_fusion.2
  2.2 0.1 fusion.16
  2.3 0.7 fusion.20
  4.3 1.4 pad_add_fusion
  5.6 0.1 fusion.18
  5.7 154.9 %conditional.2 = (bf16[128,5120]{1,0:T(8,128)(2,1)}, bf16[1,64,5120]{2,1,0:T(8,128)(2,1)}, bf16[1,64,5120]{2,1,0:T(8,128)(2,1)}) conditional(s32[]{:T(128)} %convert_element_type.50, (bf16[1,64,5120]{2,1,0:T(8,128)(2,1)}, bf16[1,64,5120]{2,1,0:T(8,128)(2,1)}, s32[16]{0:T(128)S(1)}, bf16[128,5120]{1,0:T(8,128)(2,1)}, s32[16]{0:T(128)S(1)}, ...), branch_computations={%region_4.5_spmd, %region_5.9_spmd} | conditional | flops 447628544 | bytes 59691400
  5.7 16.1 %all_to_all.50.refs_0_ = bf16[8,8,5120]{2,1,0:T(8,128)(2,1)S(1)} all-to-all(bf16[8,8,5120]{2,1,0:T(8,128)(2,1)} %bitcast.56), channel_id=1, replica_groups={{0,1,2,3,4,5,6,7},{8,9,10,11,12,13,14,15},{16,17,18,19,20,21,22,23},{24..., dimensions={0} | all-to-all | bytes 1310720 | tf_op jit(solution)/shard_map/cond/branch_1_fun/all_to_all | solution.py:188
  21.9 3.5 %all-to-all-start = ((bf16[8,8,5120]{2,1,0:T(8,128)(2,1)}), bf16[8,8,5120]{2,1,0:T(8,128)(2,1)S(1)}, u32[]{:S(2)}, u32[]{:S(2)}) async-start(bf16[8,8,5120]{2,1,0:T(8,128)(2,1)} %bitcast.9), calls=%async_computation | async-start | bytes 1310720 | tf_op jit(solution)/shard_map/cond/branch_1_fun/all_to_all | solution.py:188
  25.4 0.1 reduce_sum.37
  25.5 0.1 dynamic_slice.10
  25.6 0.1 dynamic_slice.9
  25.7 0.1 dynamic_slice.8
  25.8 0.1 select_reduce_fusion.1.index_ref
  25.9 0.2 select_reduce_fusion
  26.1 0.6 branch_1_fun.10
  26.7 2.7 %collective-permute-start.1 = (bf16[4,8,5120]{2,1,0:T(8,128)(2,1)S(1)}, bf16[4,8,5120]{2,1,0:T(8,128)(2,1)S(1)}, u32[]{:S(2)}, u32[]{:S(2)}) collective-permute-start(bf16[4,8,5120]{2,1,0:T(8,128)(2,1)S(1)} %branch_1_fun.10), channel_id=1, source_target_pairs={{0,8},{1,9},{2,10},{3,11},{4,12},{5,13},{6,14},{7,15},{8,0},{9,1},... | collective-permute-start | bytes 983048 | tf_op jit(solution)/shard_map/cond/branch_1_fun/ppermute | solution.py:191
  29.4 0.1 broadcast_select_fusion
  29.5 15.3 %collective-permute-done.1.refs_1_ = bf16[4,8,5120]{2,1,0:T(8,128)(2,1)S(1)} collective-permute-done((bf16[4,8,5120]{2,1,0:T(8,128)(2,1)S(1)}, bf16[4,8,5120]{2,1,0:T(8,128)(2,1)S(1)}, u32[]{:S(2)}, u32[]{:S(2)}) %collective-permute-start.1) | collective-permute-done | bytes 327712 | tf_op jit(solution)/shard_map/cond/branch_1_fun/ppermute | solution.py:191
  44.7 1.6 branch_1_fun.11
  46.3 0.0 all-to-all-done.refs_0_
  46.3 3.5 %all-to-all-start.3 = ((bf16[8,8,5120]{2,1,0:T(8,128)(2,1)}), bf16[8,8,5120]{2,1,0:T(8,128)(2,1)S(1)}, u32[]{:S(2)}, u32[]{:S(2)}) async-start(bf16[8,8,5120]{2,1,0:T(8,128)(2,1)} %branch_1_fun.11), calls=%async_computation.3 | async-start | bytes 1310720 | tf_op jit(solution)/shard_map/cond/branch_1_fun/all_to_all | solution.py:194
  49.9 0.6 branch_1_fun.8
  50.5 0.0 copy-start.1
  50.5 3.0 %collective-permute-start = (bf16[4,8,5120]{2,1,0:T(8,128)(2,1)S(1)}, bf16[4,8,5120]{2,1,0:T(8,128)(2,1)S(1)}, u32[]{:S(2)}, u32[]{:S(2)}) collective-permute-start(bf16[4,8,5120]{2,1,0:T(8,128)(2,1)S(1)} %branch_1_fun.8), channel_id=1, source_target_pairs={{0,8},{1,9},{2,10},{3,11},{4,12},{5,13},{6,14},{7,15},{8,0},{9,1},... | collective-permute-start | bytes 983048 | tf_op jit(solution)/shard_map/cond/branch_1_fun/ppermute | solution.py:191
  53.5 11.5 %collective-permute-done.refs_1_ = bf16[4,8,5120]{2,1,0:T(8,128)(2,1)S(1)} collective-permute-done((bf16[4,8,5120]{2,1,0:T(8,128)(2,1)S(1)}, bf16[4,8,5120]{2,1,0:T(8,128)(2,1)S(1)}, u32[]{:S(2)}, u32[]{:S(2)}) %collective-permute-start) | collective-permute-done | bytes 327712 | tf_op jit(solution)/shard_map/cond/branch_1_fun/ppermute | solution.py:191
  65.0 1.6 branch_1_fun.9
  66.6 0.5 all-to-all-done.3
  67.0 6.7 %all-to-all-start.1 = ((bf16[8,8,5120]{2,1,0:T(8,128)(2,1)}), bf16[8,8,5120]{2,1,0:T(8,128)(2,1)S(1)}, u32[]{:S(2)}, u32[]{:S(2)}) async-start(bf16[8,8,5120]{2,1,0:T(8,128)(2,1)} %branch_1_fun.9), calls=%async_computation.1 | async-start | bytes 1310720 | tf_op jit(solution)/shard_map/cond/branch_1_fun/all_to_all | solution.py:194
  73.8 0.0 copy-done.1
  73.8 3.3 %fusion.1 = bf16[8,8,5120]{2,1,0:T(8,128)(2,1)} fusion(bf16[128,5120]{1,0:T(8,128)(2,1)S(1)} %copy-done.1, bf16[128,5120]{1,0:T(8,128)(2,1)} %get-tuple-element.47, bf16[8,8,5120]{2,1,0:T(8,128)(2,1)S(1)} %all-to-all-done.3), kind=kOutput, calls=%fused_computation.4 | convolution fusion | flops 168108032 | bytes 3932160 | tf_op jit(solution)/shard_map/cond/branch_1_fun/tr,td->rd/dot_general | solution.py:113
  77.1 6.9 %all-to-all-done.1 = bf16[8,8,5120]{2,1,0:T(8,128)(2,1)S(1)} async-done(((bf16[8,8,5120]{2,1,0:T(8,128)(2,1)}), bf16[8,8,5120]{2,1,0:T(8,128)(2,1)S(1)}, u32[]{:S(2)}, u32[]{:S(2)}) %all-to-all-start.1) | async-done | bytes 655392 | tf_op jit(solution)/shard_map/cond/branch_1_fun/all_to_all | solution.py:194
  84.0 3.5 %all-to-all-start.6 = ((bf16[8,8,5120]{2,1,0:T(8,128)(2,1)}), bf16[8,8,5120]{2,1,0:T(8,128)(2,1)S(1)}, u32[]{:S(2)}, u32[]{:S(2)}) async-start(bf16[8,8,5120]{2,1,0:T(8,128)(2,1)} %fusion.1), calls=%async_computation.6 | async-start | bytes 1310720 | tf_op jit(solution)/shard_map/cond/branch_1_fun/all_to_all | solution.py:188
  87.6 0.0 copy-start.3
  87.6 0.6 convolution_convert_fusion.3
  88.2 0.7 copy-done.3
  88.9 1.2 fusion
  90.1 7.7 %all-to-all-done.6.refs_1_.refs_2_ = bf16[8,8,5120]{2,1,0:T(8,128)(2,1)S(1)} async-done(((bf16[8,8,5120]{2,1,0:T(8,128)(2,1)}), bf16[8,8,5120]{2,1,0:T(8,128)(2,1)S(1)}, u32[]{:S(2)}, u32[]{:S(2)}) %all-to-all-start.6) | async-done | bytes 655392 | tf_op jit(solution)/shard_map/cond/branch_1_fun/all_to_all | solution.py:188
  97.8 3.5 %all-to-all-start.4 = ((bf16[8,8,5120]{2,1,0:T(8,128)(2,1)}), bf16[8,8,5120]{2,1,0:T(8,128)(2,1)S(1)}, u32[]{:S(2)}, u32[]{:S(2)}) async-start(bf16[8,8,5120]{2,1,0:T(8,128)(2,1)} %fusion), calls=%async_computation.4 | async-start | bytes 1310720 | tf_op jit(solution)/shard_map/cond/branch_1_fun/all_to_all | solution.py:188
  101.3 0.8 branch_1_fun.14
  102.1 3.2 %collective-permute-start.3 = (bf16[4,8,5120]{2,1,0:T(8,128)(2,1)S(1)}, bf16[4,8,5120]{2,1,0:T(8,128)(2,1)S(1)}, u32[]{:S(2)}, u32[]{:S(2)}) collective-permute-start(bf16[4,8,5120]{2,1,0:T(8,128)(2,1)S(1)} %branch_1_fun.14), channel_id=1, source_target_pairs={{0,8},{1,9},{2,10},{3,11},{4,12},{5,13},{6,14},{7,15},{8,0},{9,1},... | collective-permute-start | bytes 983048 | tf_op jit(solution)/shard_map/cond/branch_1_fun/ppermute | solution.py:197
  105.3 0.6 dynamic_slice.11
  105.9 0.6 compare_select_fusion.refs_1_
  106.6 9.9 %collective-permute-done.3.refs_3_ = bf16[4,8,5120]{2,1,0:T(8,128)(2,1)S(1)} collective-permute-done((bf16[4,8,5120]{2,1,0:T(8,128)(2,1)S(1)}, bf16[4,8,5120]{2,1,0:T(8,128)(2,1)S(1)}, u32[]{:S(2)}, u32[]{:S(2)}) %collective-permute-start.3) | collective-permute-done | bytes 327712 | tf_op jit(solution)/shard_map/cond/branch_1_fun/ppermute | solution.py:197
  116.4 1.8 %branch_1_fun.15 = bf16[8,8,5120]{2,1,0:T(8,128)(2,1)} custom-call(s32[8]{0:T(128)S(1)} %get-tuple-element.65.refs_0_, s32[4]{0:T(128)S(1)} %compare_select_fusion.refs_1_, bf16[8,8,5120]{2,1,0:T(8,128)(2,1)S(1)} %all-to-all-done.6.refs_1_.refs_2_, bf16[4,8,5120]{2,1,0:T(8,128)(2,1)S(1)} %collective-permute-done.3.refs_3_), custom_call_target="tpu_custom_call" | custom-call | tf_op jit(solution)/shard_map/cond/branch_1_fun/pallas_call | solution.py:100
  118.3 0.2 all-to-all-done.4.refs_1_.refs_2_
  118.5 7.2 %all-to-all-start.7 = ((bf16[8,8,5120]{2,1,0:T(8,128)(2,1)}), bf16[8,8,5120]{2,1,0:T(8,128)(2,1)}, u32[]{:S(2)}, u32[]{:S(2)}) async-start(bf16[8,8,5120]{2,1,0:T(8,128)(2,1)} %branch_1_fun.15), calls=%async_computation.7 | async-start | bytes 1310720 | tf_op jit(solution)/shard_map/cond/branch_1_fun/all_to_all | solution.py:201
  125.7 0.8 branch_1_fun.12
  126.5 3.4 %collective-permute-start.2 = (bf16[4,8,5120]{2,1,0:T(8,128)(2,1)S(1)}, bf16[4,8,5120]{2,1,0:T(8,128)(2,1)S(1)}, u32[]{:S(2)}, u32[]{:S(2)}) collective-permute-start(bf16[4,8,5120]{2,1,0:T(8,128)(2,1)S(1)} %branch_1_fun.12), channel_id=1, source_target_pairs={{0,8},{1,9},{2,10},{3,11},{4,12},{5,13},{6,14},{7,15},{8,0},{9,1},... | collective-permute-start | bytes 983048 | tf_op jit(solution)/shard_map/cond/branch_1_fun/ppermute | solution.py:197
  129.9 11.0 %collective-permute-done.2.refs_3_ = bf16[4,8,5120]{2,1,0:T(8,128)(2,1)S(1)} collective-permute-done((bf16[4,8,5120]{2,1,0:T(8,128)(2,1)S(1)}, bf16[4,8,5120]{2,1,0:T(8,128)(2,1)S(1)}, u32[]{:S(2)}, u32[]{:S(2)}) %collective-permute-start.2) | collective-permute-done | bytes 327712 | tf_op jit(solution)/shard_map/cond/branch_1_fun/ppermute | solution.py:197
  140.9 1.8 %branch_1_fun.13 = bf16[8,8,5120]{2,1,0:T(8,128)(2,1)} custom-call(s32[8]{0:T(128)S(1)} %get-tuple-element.65.refs_0_, s32[4]{0:T(128)S(1)} %compare_select_fusion.refs_1_, bf16[8,8,5120]{2,1,0:T(8,128)(2,1)S(1)} %all-to-all-done.4.refs_1_.refs_2_, bf16[4,8,5120]{2,1,0:T(8,128)(2,1)S(1)} %collective-permute-done.2.refs_3_), custom_call_target="tpu_custom_call" | custom-call | tf_op jit(solution)/shard_map/cond/branch_1_fun/pallas_call | solution.py:100
  142.7 0.3 all-to-all-done.7
  143.1 7.2 %all-to-all-start.5 = ((bf16[8,8,5120]{2,1,0:T(8,128)(2,1)}), bf16[8,8,5120]{2,1,0:T(8,128)(2,1)}, u32[]{:S(2)}, u32[]{:S(2)}) async-start(bf16[8,8,5120]{2,1,0:T(8,128)(2,1)} %branch_1_fun.13), calls=%async_computation.5 | async-start | bytes 1310720 | tf_op jit(solution)/shard_map/cond/branch_1_fun/all_to_all | solution.py:201
  150.3 1.6 fusion.4
  151.9 8.8 %all-to-all-done.5 = bf16[8,8,5120]{2,1,0:T(8,128)(2,1)} async-done(((bf16[8,8,5120]{2,1,0:T(8,128)(2,1)}), bf16[8,8,5120]{2,1,0:T(8,128)(2,1)}, u32[]{:S(2)}, u32[]{:S(2)}) %all-to-all-start.5) | async-done | bytes 655392 | tf_op jit(solution)/shard_map/cond/branch_1_fun/all_to_all | solution.py:201
  160.7 2.0 %copy.27 = bf16[1,64,5120]{2,1,0:T(8,128)(2,1)} copy(bf16[1,64,5120]{2,1,0:T(8,128)(2,1)} %get-tuple-element.77) | data formatting | bytes 1310720
  162.6 2.0 %copy.28 = bf16[1,64,5120]{2,1,0:T(8,128)(2,1)} copy(bf16[1,64,5120]{2,1,0:T(8,128)(2,1)} %get-tuple-element.78) | data formatting | bytes 1310720
  (2 shorter events, 0.0 us)
Async XLA Ops:
  21.9 24.4 %all-to-all-start = ((bf16[8,8,5120]{2,1,0:T(8,128)(2,1)}), bf16[8,8,5120]{2,1,0:T(8,128)(2,1)S(1)}, u32[]{:S(2)}, u32[]{:S(2)}) async-start(bf16[8,8,5120]{2,1,0:T(8,128)(2,1)} %bitcast.9), calls=%async_computation | async-start | bytes 1310720 | tf_op jit(solution)/shard_map/cond/branch_1_fun/all_to_all | solution.py:188
  26.7 18.0 %collective-permute-start.1 = (bf16[4,8,5120]{2,1,0:T(8,128)(2,1)S(1)}, bf16[4,8,5120]{2,1,0:T(8,128)(2,1)S(1)}, u32[]{:S(2)}, u32[]{:S(2)}) collective-permute-start(bf16[4,8,5120]{2,1,0:T(8,128)(2,1)S(1)} %branch_1_fun.10), channel_id=1, source_target_pairs={{0,8},{1,9},{2,10},{3,11},{4,12},{5,13},{6,14},{7,15},{8,0},{9,1},... | collective-permute-start | bytes 983048 | tf_op jit(solution)/shard_map/cond/branch_1_fun/ppermute | solution.py:191
  46.3 20.7 %all-to-all-start.3 = ((bf16[8,8,5120]{2,1,0:T(8,128)(2,1)}), bf16[8,8,5120]{2,1,0:T(8,128)(2,1)S(1)}, u32[]{:S(2)}, u32[]{:S(2)}) async-start(bf16[8,8,5120]{2,1,0:T(8,128)(2,1)} %branch_1_fun.11), calls=%async_computation.3 | async-start | bytes 1310720 | tf_op jit(solution)/shard_map/cond/branch_1_fun/all_to_all | solution.py:194
  50.5 23.3 %copy-start.1 = (bf16[128,5120]{1,0:T(8,128)(2,1)S(1)}, bf16[128,5120]{1,0:T(8,128)(2,1)}, u32[]{:S(2)}) copy-start(bf16[128,5120]{1,0:T(8,128)(2,1)} %get-tuple-element.44) | copy-start | bytes 3932164 | tf_op jit(solution)/shard_map/conditional
  50.5 14.5 %collective-permute-start = (bf16[4,8,5120]{2,1,0:T(8,128)(2,1)S(1)}, bf16[4,8,5120]{2,1,0:T(8,128)(2,1)S(1)}, u32[]{:S(2)}, u32[]{:S(2)}) collective-permute-start(bf16[4,8,5120]{2,1,0:T(8,128)(2,1)S(1)} %branch_1_fun.8), channel_id=1, source_target_pairs={{0,8},{1,9},{2,10},{3,11},{4,12},{5,13},{6,14},{7,15},{8,0},{9,1},... | collective-permute-start | bytes 983048 | tf_op jit(solution)/shard_map/cond/branch_1_fun/ppermute | solution.py:191
  67.0 17.0 %all-to-all-start.1 = ((bf16[8,8,5120]{2,1,0:T(8,128)(2,1)}), bf16[8,8,5120]{2,1,0:T(8,128)(2,1)S(1)}, u32[]{:S(2)}, u32[]{:S(2)}) async-start(bf16[8,8,5120]{2,1,0:T(8,128)(2,1)} %branch_1_fun.9), calls=%async_computation.1 | async-start | bytes 1310720 | tf_op jit(solution)/shard_map/cond/branch_1_fun/all_to_all | solution.py:194
  84.0 13.7 %all-to-all-start.6 = ((bf16[8,8,5120]{2,1,0:T(8,128)(2,1)}), bf16[8,8,5120]{2,1,0:T(8,128)(2,1)S(1)}, u32[]{:S(2)}, u32[]{:S(2)}) async-start(bf16[8,8,5120]{2,1,0:T(8,128)(2,1)} %fusion.1), calls=%async_computation.6 | async-start | bytes 1310720 | tf_op jit(solution)/shard_map/cond/branch_1_fun/all_to_all | solution.py:188
  87.6 1.3 copy-start.3
  97.8 20.7 %all-to-all-start.4 = ((bf16[8,8,5120]{2,1,0:T(8,128)(2,1)}), bf16[8,8,5120]{2,1,0:T(8,128)(2,1)S(1)}, u32[]{:S(2)}, u32[]{:S(2)}) async-start(bf16[8,8,5120]{2,1,0:T(8,128)(2,1)} %fusion), calls=%async_computation.4 | async-start | bytes 1310720 | tf_op jit(solution)/shard_map/cond/branch_1_fun/all_to_all | solution.py:188
  102.1 14.3 %collective-permute-start.3 = (bf16[4,8,5120]{2,1,0:T(8,128)(2,1)S(1)}, bf16[4,8,5120]{2,1,0:T(8,128)(2,1)S(1)}, u32[]{:S(2)}, u32[]{:S(2)}) collective-permute-start(bf16[4,8,5120]{2,1,0:T(8,128)(2,1)S(1)} %branch_1_fun.14), channel_id=1, source_target_pairs={{0,8},{1,9},{2,10},{3,11},{4,12},{5,13},{6,14},{7,15},{8,0},{9,1},... | collective-permute-start | bytes 983048 | tf_op jit(solution)/shard_map/cond/branch_1_fun/ppermute | solution.py:197
  118.5 24.6 %all-to-all-start.7 = ((bf16[8,8,5120]{2,1,0:T(8,128)(2,1)}), bf16[8,8,5120]{2,1,0:T(8,128)(2,1)}, u32[]{:S(2)}, u32[]{:S(2)}) async-start(bf16[8,8,5120]{2,1,0:T(8,128)(2,1)} %branch_1_fun.15), calls=%async_computation.7 | async-start | bytes 1310720 | tf_op jit(solution)/shard_map/cond/branch_1_fun/all_to_all | solution.py:201
  126.5 14.4 %collective-permute-start.2 = (bf16[4,8,5120]{2,1,0:T(8,128)(2,1)S(1)}, bf16[4,8,5120]{2,1,0:T(8,128)(2,1)S(1)}, u32[]{:S(2)}, u32[]{:S(2)}) collective-permute-start(bf16[4,8,5120]{2,1,0:T(8,128)(2,1)S(1)} %branch_1_fun.12), channel_id=1, source_target_pairs={{0,8},{1,9},{2,10},{3,11},{4,12},{5,13},{6,14},{7,15},{8,0},{9,1},... | collective-permute-start | bytes 983048 | tf_op jit(solution)/shard_map/cond/branch_1_fun/ppermute | solution.py:197
  143.1 17.6 %all-to-all-start.5 = ((bf16[8,8,5120]{2,1,0:T(8,128)(2,1)}), bf16[8,8,5120]{2,1,0:T(8,128)(2,1)}, u32[]{:S(2)}, u32[]{:S(2)}) async-start(bf16[8,8,5120]{2,1,0:T(8,128)(2,1)} %branch_1_fun.13), calls=%async_computation.5 | async-start | bytes 1310720 | tf_op jit(solution)/shard_map/cond/branch_1_fun/all_to_all | solution.py:201
